TPU v7x, 256 devices: a whole 4x4x8 slice. The times are simulated.
256 devices in a mesh: clip: 16 (over z, x_lo), tm: 16 (over y, x_hi, core).
Axes of the slice: x: 4 (x_hi: 2, x_lo: 2; x = x_hi * 2 + x_lo), y: 4, z: 8, core: 2. Of those that a mesh axis runs over, the one named last changes fastest.
Arguments:
- clip_embed: bfloat16 [6144, 512], P('clip'), may hold values from -0.1875 to 0.1875
- seg_feats: bfloat16 [16, 6144, 512], P('tm', 'clip'), may hold values from -1 to 1
- pair_index: int32 [16, 6144], P('tm', 'clip'), may hold values from 0 to 6143, as said below
Outputs:
- row_loss: float32 [16, 6144], P('tm', 'clip')
- grad_seg: float32 [16, 6144, 512], P('tm', 'clip')
- grad_clip: float32 [6144, 512], P('clip')
Inputs may be any that keep to these rules, and one draw needn't show every extreme that they name: pair_index pairs the rows of each segment: pair_index[t, i] != i and pair_index[t, pair_index[t, i]] = i.
All inputs are finite; a program needn't handle non-finite values.
Results may differ from a plain program's by a relative error of at most 0.0029.
Values may be sent and summed in bfloat16 or wider, within the bound.
A program may use at most 128 MiB of HBM per device.

v0:
```python
import jax
import jax.numpy as jnp
from jax import lax
from jax.sharding import PartitionSpec as P

logit_scale = 14.0
norm_eps = 1e-06


def embed(clip_embed, features):
    summed = clip_embed.astype(jnp.float32) + features.astype(jnp.float32)
    factor = lax.rsqrt(jnp.sum(summed * summed, 1, keepdims=True) + summed.shape[1] * norm_eps)
    return (summed, factor, (summed * factor).astype(jnp.bfloat16))


def scores(left_rows, right_rows):
    return jnp.einsum("re,ce->rc", left_rows, right_rows, preferred_element_type=jnp.float32)


def pull_rows(weights, block):
    return jnp.dot(
        weights,
        block.astype(jnp.float32),
        precision=lax.Precision.HIGHEST,
        preferred_element_type=jnp.float32,
    )


def exponent(score):
    return jnp.exp(logit_scale * (score - 1.0))


def pick_rows(partners, col_start, width):
    local_index = partners - col_start
    inside = (local_index >= 0) & (local_index < width)
    return (jnp.clip(local_index, 0, width - 1), inside)


def finish(summed, factor, field):
    grad_unit = logit_scale * field
    along = jnp.sum(summed * grad_unit, 1, keepdims=True)
    return factor * grad_unit - factor**3 * summed * along


def on_device(clip_embed, seg_feats, pair_index):
    summed, factor, unit = embed(clip_embed, seg_feats[0])
    partners = pair_index[0]
    row_count = unit.shape[0]
    width_e = unit.shape[1]
    device = lax.axis_index("clip")
    own_rows = device * row_count + jnp.arange(row_count, dtype=jnp.int32)
    start_pair = (jnp.zeros((row_count,), jnp.float32), jnp.zeros((row_count,), jnp.float32))
    shard_rows = lax.all_gather(unit, "clip", axis=0, tiled=True)
    width = min(row_count, shard_rows.shape[0])
    stacked = shard_rows.reshape(-1, width, width_e)
    offsets = width * jnp.arange(stacked.shape[0], dtype=jnp.int32)

    def first_advance(current, item):
        column_block, offset = item
        score = scores(unit, column_block)
        columns = offset + jnp.arange(width, dtype=jnp.int32)
        terms = jnp.where(own_rows[:, None] != columns[None, :], exponent(score), 0.0)
        where_at, inside = pick_rows(partners, offset, width)
        picked = jnp.take_along_axis(score, where_at[:, None], 1)[:, 0]
        return ((current[0] + jnp.sum(terms, 1), current[1] + jnp.where(inside, picked, 0.0)), None)

    result, ignored = lax.scan(first_advance, start_pair, (stacked, offsets))
    totals, positive = result
    inverse = 1.0 / totals
    shard_pair = (
        lax.all_gather(unit, "clip", axis=0, tiled=True),
        lax.all_gather(totals.astype(jnp.bfloat16), "clip", axis=0, tiled=True).astype(jnp.float32),
    )
    second_width = min(row_count, shard_pair[0].shape[0])
    stacked = shard_pair[0].reshape(-1, second_width, width_e)
    stacked_totals = shard_pair[1].reshape(-1, second_width)
    offsets = second_width * jnp.arange(stacked.shape[0], dtype=jnp.int32)

    def second_advance(current, item):
        column_block, column_totals, offset = item
        score = scores(unit, column_block)
        columns = offset + jnp.arange(second_width, dtype=jnp.int32)
        terms = jnp.where(own_rows[:, None] != columns[None, :], exponent(score), 0.0)
        weights = terms * (inverse[:, None] + (1.0 / column_totals)[None, :])
        pulled = pull_rows(weights, column_block)
        where_at, inside = pick_rows(partners, offset, second_width)
        chosen = jnp.take(column_block, where_at, axis=0).astype(jnp.float32)
        return (current + pulled - 2.0 * jnp.where(inside[:, None], chosen, 0.0), None)

    result, ignored = lax.scan(
        second_advance,
        jnp.zeros((row_count, width_e), jnp.float32),
        (stacked, stacked_totals, offsets),
    )
    row_loss = logit_scale * (1.0 - positive) + jnp.log(totals)
    grad_seg = finish(summed, factor, result)
    grad_clip = lax.psum(grad_seg, "tm")
    return (row_loss[None], grad_seg[None], grad_clip)


def solution(mesh):
    placed = (P("clip", None), P("tm", "clip", None), P("tm", "clip"))
    return jax.shard_map(
        on_device,
        mesh=mesh,
        in_specs=placed,
        out_specs=(P("tm", "clip"), P("tm", "clip", None), P("clip", None)),
        check_vma=False,
    )
```

profile of v0, /device:TPU:1, one launch (start us, length us, event | category | flops | bytes accessed | tf_op | source)
XLA Modules:
  0.0 586.2 jit_solution(2581798895463444962)
XLA Ops:
  11.3 143.5 %all-gather.3.cloned.1.call-done = bf16[6144,512]{1,0:T(8,128)(2,1)} async-done(((bf16[384,512]{1,0:T(8,128)(2,1)}), bf16[6144,512]{1,0:T(8,128)(2,1)}) %all-gather.3.cloned.1.call-update) | async-done | bytes 6291472 | tf_op jit(solution)/shard_map/all_gather | solution.py:53
  154.8 122.7 %while.28 = (s32[]{:T(128)}, f32[384]{0:T(512)S(1)}, f32[384]{0:T(512)S(1)}, s32[16]{0:T(128)S(1)}, bf16[16,384,512]{2,1,0:T(8,128)(2,1)}, /*index=5*/bf16[384,5...) while((s32[]{:T(128)}, f32[384]{0:T(512)S(1)}, f32[384]{0:T(512)S(1)}, ...), condition=%wide.region_3.4_spmd.clone, body=%wide.region_1.3_spmd.clone.sunk | while | flops 151743744 | bytes 1419415 | solution.py:67
  158.3 3.5 gather_fusion
  166.0 3.5 gather_fusion
  173.7 3.5 gather_fusion
  181.3 3.5 gather_fusion
  189.0 3.5 gather_fusion
  196.7 3.5 gather_fusion
  204.4 3.5 gather_fusion
  212.0 3.5 gather_fusion
  219.7 3.5 gather_fusion
  227.4 3.5 gather_fusion
  235.1 3.5 gather_fusion
  242.7 3.5 gather_fusion
  250.4 3.5 gather_fusion
  258.1 3.5 gather_fusion
  265.8 3.5 gather_fusion
  273.4 3.5 gather_fusion
  277.6 25.7 %all-gather = bf16[16,1,384]{2,1,0:T(2,128)(2,1)S(1)} all-gather(bf16[1,1,384]{2,1,0:T(2,128)(2,1)S(1)} %reshape.151), channel_id=1, replica_groups=mesh['clip'=16,'tm'=16] {'clip'}, dimensions={0}, use_global_device_ids=true | all-gather | bytes 13056 | tf_op jit(solution)/shard_map/all_gather | solution.py:72
  303.3 120.8 %while.29 = (s32[]{:T(128)}, f32[384,512]{1,0:T(8,128)S(1)}, s32[16]{0:T(128)S(1)}, bf16[16,384,512]{2,1,0:T(8,128)(2,1)}, bf16[384,512]{1,0:T(8,128)(2,1)}, /*i...) while((s32[]{:T(128)}, f32[384,512]{1,0:T(8,128)S(1)}, ...), condition=%wide.region_5.6_spmd.clone, body=%wide.region_4.5_spmd.clone.sunk | while | flops 1059233152 | bytes 5925535 | solution.py:90
  306.3 2.1 gather_fusion.1
  313.9 2.1 gather_fusion.1
  321.4 2.1 gather_fusion.1
  329.0 2.1 gather_fusion.1
  344.1 2.1 gather_fusion.1
  351.6 2.1 gather_fusion.1
  359.2 2.1 gather_fusion.1
  366.7 2.1 gather_fusion.1
  374.3 2.1 gather_fusion.1
  381.8 2.1 gather_fusion.1
  397.0 2.1 gather_fusion.1
  426.1 151.2 %all-reduce.2.cloned.1.call-done = f32[384,512]{1,0:T(8,128)} async-done(((f32[384,512]{1,0:T(8,128)}), f32[384,512]{1,0:T(8,128)}) %all-reduce.2.cloned.1.call-update) | async-done | bytes 786448 | tf_op jit(solution)/shard_map/psum | solution.py:97
  (332 shorter events, 171.4 us)
Async XLA Ops:
  7.2 147.6 %all-gather.3.cloned.1.call-start = ((), (), s32[]{:S(2)}) async-start(), calls=%async_computation | async-start | bytes 6684672 | tf_op jit(solution)/shard_map/all_gather | solution.py:53
  10.6 566.7 %all-reduce.2.cloned.1.call-start = ((), (), s32[]{:S(2)}) async-start(), calls=%async_computation.1 | async-start | bytes 1572864 | tf_op jit(solution)/shard_map/psum | solution.py:97
  303.3 120.8 %copy-start = (bf16[384,512]{1,0:T(8,128)(2,1)S(1)}, bf16[384,512]{1,0:T(8,128)(2,1)}, u32[]{:S(2)}) copy-start(bf16[384,512]{1,0:T(8,128)(2,1)} %param.7) | copy-start | bytes 1179652
  303.3 120.8 %copy-start.1 = (bf16[1,384,512]{2,1,0:T(8,128)(2,1)S(1)}, bf16[1,384,512]{2,1,0:T(8,128)(2,1)}, u32[]{:S(2)}) copy-start(bf16[1,384,512]{2,1,0:T(8,128)(2,1)} %param.8) | copy-start | bytes 1179652
Sparse Core Ops, SparseCore 0:
  10.7 144.0 all-gather.2
  425.7 151.5 all-reduce.1
where the time goes:
time: 589 us; the launch traced here: 586 us
  waiting for transfers between devices  295 us (50%)
  local copies, waits for them, and re-layouts  127 us (22%)
  matrix products  63.9 us (11%)
  other arithmetic  58.7 us (10%)
  blocking collectives  25.7 us (4%)
  between operations  14.1 us (2%)
    psum x1, waiting for transfers between devices, on_device(): grad_clip = lax.psum(grad_seg, 'tm')  151 us
    all_gather x1, waiting for transfers between devices, on_device(): shard_rows = lax.all_gather(unit, 'clip', axis=0, tiled=True)  143 us
    gather x16, local copies, waits for them, and re-layouts, first_advance(): picked = jnp.take_along_axis(score, where_at[:, None], 1)[:, 0]  55.5 us
    dot_general x32, matrix products, scores(): jnp.einsum('re,ce->rc', left_rows, right_rows, preferred_element_type=jnp...  47.6 us
    gather x16, local copies, waits for them, and re-layouts, second_advance(): chosen = jnp.take(column_block, where_at, axis=0).astype(jnp.float32)  33 us
    all_gather x1, blocking collectives, on_device(): lax.all_gather(totals.astype(jnp.bfloat16), 'clip', axis=0, tiled=True)  25.7 us
    dynamic_slice x32, local copies, waits for them, and re-layouts, on_device(): result, ignored = lax.scan(first_advance, start_pair, (stacked, offsets))  19.2 us
    squeeze x16, local copies, waits for them, and re-layouts, on_device(): result, ignored = lax.scan(first_advance, start_pair, (stacked, offsets))  16.5 us
  transfers between devices with their start and end apart: 2, of which 2 were waited for; matrix products, arithmetic and copies ran while one was open for 0% of the time, Pallas kernels for 0%

commit v1 on v0

v1 whole, which is shorter than its diff:
```python
import functools
import math

import jax
import jax.numpy as jnp
from jax import lax
from jax.experimental import pallas as pl
from jax.experimental.pallas import tpu as pltpu
from jax.sharding import PartitionSpec as P

MESH = pl.DeviceIdType.MESH
logit_scale = 14.0
norm_eps = 1e-06
exp2_scale = logit_scale * math.log2(math.e)

ZS = 8
ROWS = 384
HALF = ROWS // 2
PAIR = 2 * ROWS
E = 512
PEERS = 8
PIECE = ROWS // PEERS
STEPS = ZS


def remote(src, dst, send_sem, recv_sem, device):
    return pltpu.make_async_remote_copy(
        src_ref=src, dst_ref=dst, send_sem=send_sem, recv_sem=recv_sem,
        device_id=device, device_id_type=MESH,
    )


def dot(a, b):
    return jnp.dot(a, b, preferred_element_type=jnp.float32)


def kernel(
    clip_ref, feat_ref, pair_ref,
    loss_out, seg_out, clip_out,
    u_all, ut_all, expo_all, tot_all, unit_t, stage, raw_clip, raw_feat, partner, totals,
    pull_one, pull_pos, acc, summed_t, ret_stage, ret, sib_grad, loss_stage, loss_ret,
    rs_send, rs_buf, gathered,
    swap_s, swap_r, ring_s, ring_r, sib_s, sib_r, tot_s, tot_r, ret_s, ret_r, grad_s, grad_r,
    rs_s, rs_r, ag_s, ag_r, fin_s, fin_r,
):
    clip = lax.axis_index("clip")
    tm = lax.axis_index("tm")
    z, x = clip // 2, lax.rem(clip, 2)
    peer, core = tm // 2, lax.rem(tm, 2)
    stays = x == core
    moves = x != core

    def at(zz, xx, pp, cc):
        return (zz * 2 + xx, pp * 2 + cc)

    def ring(offset):
        return lax.rem(z + offset + ZS, ZS)

    sibling = at(z, x, peer, 1 - core)
    swapped = at(z, 1 - x, peer, 1 - core)

    barrier = pltpu.get_barrier_semaphore()

    def greet(device):
        pl.semaphore_signal(barrier, inc=1, device_id=device, device_id_type=MESH)

    for dz in range(ZS):
        for dc in range(2):
            if dz or dc:
                greet(at(ring(dz), x, peer, lax.rem(core + dc, 2)))

    @pl.when(moves)
    def _():
        greet(swapped)
        for d in range(1, PEERS):
            greet(at(z, x, lax.rem(peer + d, PEERS), core))

    summed = clip_ref[...].astype(jnp.float32) + feat_ref[0].astype(jnp.float32)
    factor = lax.rsqrt(jnp.sum(summed * summed, 1, keepdims=True) + E * norm_eps)
    unit = (summed * factor).astype(jnp.bfloat16)

    def half(zz, block, which):
        return u_all.at[zz, pl.ds(pl.multiple_of(block * ROWS + which * HALF, HALF), HALF)]

    def swap_copies():
        return [
            remote(stage.at[pl.ds(0, HALF)], half(z, x, 0), swap_s.at[0], swap_r.at[0], swapped),
            remote(stage.at[pl.ds(HALF, HALF)], half(z, x, 1), swap_s.at[1], swap_r.at[1], swapped),
            remote(pair_ref, partner, swap_s.at[2], swap_r.at[2], swapped),
            remote(feat_ref.at[0], raw_feat, swap_s.at[3], swap_r.at[3], swapped),
            remote(clip_ref, raw_clip, swap_s.at[4], swap_r.at[4], swapped),
        ]

    def swap_waits():
        copies = swap_copies()
        copies[0] = remote(stage.at[pl.ds(0, HALF)], half(z, core, 0), swap_s.at[0], swap_r.at[0], swapped)
        copies[1] = remote(stage.at[pl.ds(HALF, HALF)], half(z, core, 1), swap_s.at[1], swap_r.at[1], swapped)
        return copies

    def ring_copy(way, hop, order):
        if way == 0:
            source, target, which = ring(-hop), ring(1), order
        else:
            source, target, which = ring(hop), ring(-1), 1 - order
        ref = half(source, core, which)
        index = 2 * hop + order
        return remote(ref, ref, ring_s.at[way, index], ring_r.at[way, index], at(target, x, peer, core))

    def ring_arrival(way, hop, order):
        source, which = (ring(-hop), order) if way == 0 else (ring(hop), 1 - order)
        ref = half(source, core, which)
        index = 2 * (hop - 1) + order
        return remote(ref, ref, ring_s.at[way, index], ring_r.at[way, index], sibling), source, which

    def sib_copy(source, which):
        ref = half(source, core, which)
        return remote(ref, ref, sib_s.at[source, which], sib_r.at[source, which], sibling)

    def sib_arrival(source, which):
        ref = half(source, 1 - core, which)
        return remote(ref, ref, sib_s.at[source, which], sib_r.at[source, which], sibling)

    @pl.when(stays)
    def _():
        u_all[z, pl.ds(pl.multiple_of(core * ROWS, ROWS), ROWS), :] = unit
        raw_clip[...] = clip_ref[...]
        raw_feat[...] = feat_ref[0]
        partner[...] = pair_ref[...]
        pl.semaphore_wait(barrier, 2 * ZS - 1)

    @pl.when(moves)
    def _():
        stage[...] = unit
        pl.semaphore_wait(barrier, 2 * ZS - 1 + PEERS)
        for copy in swap_copies():
            copy.start()
        waits = swap_waits()
        for copy in waits[:3]:
            copy.wait_recv()

    for order in range(2):
        for way in range(2):
            ring_copy(way, 0, order).start()
    for which in range(2):
        sib_copy(z, which).start()

    unit_t[...] = u_all[z, pl.ds(pl.multiple_of(core * ROWS, ROWS), ROWS), :].T
    totals[...] = jnp.zeros_like(totals)
    pull_one[...] = jnp.zeros_like(pull_one)
    pull_pos[...] = jnp.zeros_like(pull_pos)

    def column_ids(zz):
        return lax.broadcasted_iota(jnp.int32, (PAIR, ROWS), 0) + zz * PAIR

    def block_of(step):
        hop = (step + 1) // 2
        return ring(jnp.where(lax.rem(step, 2) == 1, -hop, hop))

    def score_part(zz):
        score = dot(u_all[zz], unit_t[...])
        own = lax.broadcasted_iota(jnp.int32, (1, ROWS), 1) + (z * PAIR + core * ROWS)
        expo = jnp.where(column_ids(zz) != own, jnp.exp2(score * exp2_scale - exp2_scale), 0.0)
        totals[...] += jnp.sum(expo, 0, keepdims=True)
        expo_all[zz] = expo.astype(jnp.bfloat16)

    def pull_part(zz):
        ut_all[zz] = u_all[zz].T
        picked = jnp.where(column_ids(zz) == partner[...], 1.0, 0.0).astype(jnp.bfloat16)
        pull_one[...] += dot(ut_all[zz], expo_all[zz])
        pull_pos[...] += dot(ut_all[zz], picked)

    def pass_on(way, hop, order, last_hop):
        arrival, source, which = ring_arrival(way, hop, order)
        arrival.wait_recv()

        @pl.when(hop <= last_hop)
        def _():
            ring_copy(way, hop, order).start()

        sib_copy(source, which).start()

    def gather_step(step, carry):
        hop = (step + 1) // 2

        @pl.when(lax.rem(step, 2) == 1)
        def _():
            for way in range(2):
                pass_on(way, hop, 0, 3)

            @pl.when(hop <= 3)
            def _():
                for way in range(2):
                    pass_on(way, hop, 1, 2)

        zz = block_of(step)

        @pl.when(step > 0)
        def _():
            pull_part(block_of(step - 1))

        for which in range(2):
            sib_arrival(zz, which).wait_recv()
        score_part(zz)
        return carry

    lax.fori_loop(0, STEPS, gather_step, 0)

    tot_all[z, core] = totals[...]

    def total_copies():
        copies = []
        for dz in (4, 3, 5, 2, 6, 1, 7, 0):
            for dc in range(2):
                if dz or dc:
                    copies.append(remote(
                        tot_all.at[z, core], tot_all.at[z, core], tot_s.at[dz, dc], tot_r.at[z, core],
                        at(ring(dz), x, peer, lax.rem(core + dc, 2)),
                    ))
        return copies

    for copy in total_copies():
        copy.start()

    pull_part(block_of(STEPS - 1))

    inverse = 1.0 / totals[...]
    positive = jnp.sum(unit_t[...].astype(jnp.float32) * pull_pos[...], 0, keepdims=True)
    loss = logit_scale * (1.0 - positive) + jnp.log(totals[...])
    loss_copy = remote(loss_stage, loss_ret, ret_s.at[3], ret_r.at[3], swapped)

    @pl.when(stays)
    def _():
        loss_out[...] = loss

    @pl.when(moves)
    def _():
        loss_stage[...] = loss
        loss_copy.start()
        waits = swap_waits()
        for copy in waits[3:]:
            copy.wait_recv()

    acc[...] = inverse * pull_one[...] - 2.0 * pull_pos[...]
    summed_t[...] = (raw_clip[...].astype(jnp.float32) + raw_feat[...].astype(jnp.float32)).T

    def total_arrival(zz, block):
        ref = tot_all.at[zz, block]
        return remote(ref, ref, tot_s.at[0, 0], tot_r.at[zz, block], sibling)

    def second_step(step, carry):
        zz = block_of(step)

        @pl.when(step > 0)
        def _():
            total_arrival(zz, core).wait_recv()

        total_arrival(zz, 1 - core).wait_recv()
        scale = 1.0 / jnp.concatenate([tot_all[zz, 0], tot_all[zz, 1]], 1)
        scaled = (ut_all[zz].astype(jnp.float32) * scale).astype(jnp.bfloat16)
        acc[...] += dot(scaled, expo_all[zz])
        return carry

    lax.fori_loop(0, STEPS, second_step, 0)

    factor_t = lax.rsqrt(jnp.sum(summed_t[...] * summed_t[...], 0, keepdims=True) + E * norm_eps)
    width = ROWS // 3

    def ret_copy(part):
        rows = pl.ds(part * width, width)
        return remote(ret_stage.at[rows], ret.at[rows], ret_s.at[part], ret_r.at[part], swapped)

    def grad_copy(part):
        rows = pl.ds(part * width, width)
        return remote(seg_out.at[0, rows], sib_grad.at[rows], grad_s.at[part], grad_r.at[part], sibling)

    for part in range(3):
        lanes = slice(part * width, (part + 1) * width)
        grad_unit = logit_scale * acc[:, lanes]
        summed_part = summed_t[:, lanes]
        factor_part = factor_t[:, lanes]
        along = jnp.sum(summed_part * grad_unit, 0, keepdims=True)
        grad = (factor_part * grad_unit - factor_part**3 * along * summed_part).T

        @pl.when(stays)
        def _():
            seg_out[0, lanes, :] = grad
            grad_copy(part).start()

        @pl.when(moves)
        def _():
            ret_stage[lanes, :] = grad.astype(jnp.bfloat16)
            ret_copy(part).start()

    def rs_copy(piece):
        target = at(z, x, piece, core)
        rows = pl.ds(piece * PIECE, PIECE)
        return remote(rs_send.at[rows], rs_buf.at[peer], rs_s.at[piece], rs_r.at[peer], target)

    def rs_arrival(source):
        ref = rs_buf.at[source]
        return remote(ref, ref, rs_s.at[0], rs_r.at[source], sibling)

    def gathered_rows(piece):
        return gathered.at[pl.ds(pl.multiple_of(piece * PIECE, PIECE), PIECE)]

    def ag_copy(d):
        target = at(z, x, lax.rem(peer + d, PEERS), core)
        ref = gathered_rows(peer)
        return remote(ref, ref, ag_s.at[d], ag_r.at[peer], target)

    def ag_arrival(source):
        ref = gathered_rows(source)
        return remote(ref, ref, ag_s.at[0], ag_r.at[source], sibling)

    def fin_copy(piece):
        ref = gathered_rows(piece)
        return remote(ref, ref, fin_s.at[piece], fin_r.at[piece], sibling)

    @pl.when(moves)
    def _():
        loss_copy.wait_recv()
        loss_out[...] = loss_ret[...]
        first_piece = 0
        for part in range(3):
            rows = slice(part * width, (part + 1) * width)
            ret_copy(part).wait_recv()
            grad_copy(part).wait_recv()
            home = ret[rows, :].astype(jnp.float32)
            seg_out[0, rows, :] = home
            rs_send[rows, :] = (home + sib_grad[rows, :]).astype(jnp.bfloat16)
            last_piece = (part + 1) * width // PIECE
            for piece in range(first_piece, last_piece):
                @pl.when(piece != peer)
                def _():
                    rs_copy(piece).start()

                @pl.when(piece == peer)
                def _():
                    rs_buf[peer] = rs_send[piece * PIECE:(piece + 1) * PIECE, :]
            first_piece = last_piece
        for d in range(1, PEERS):
            rs_arrival(lax.rem(peer + d, PEERS)).wait_recv()
        reduced = rs_buf[0].astype(jnp.float32)
        for source in range(1, PEERS):
            reduced += rs_buf[source].astype(jnp.float32)
        gathered[pl.ds(pl.multiple_of(peer * PIECE, PIECE), PIECE), :] = reduced.astype(jnp.bfloat16)
        for d in range(1, PEERS):
            ag_copy(d).start()
        fin_copy(peer).start()
        for d in range(1, PEERS):
            source = lax.rem(peer + PEERS - d, PEERS)
            ag_arrival(source).wait_recv()
            fin_copy(source).start()

    @pl.when(stays)
    def _():
        for piece in range(PEERS):
            fin_copy(piece).wait_recv()

    clip_out[...] = gathered[...].astype(jnp.float32)

    for way in range(2):
        for hop in range(4):
            for order in range(2):
                if 2 * hop + order < 7:
                    ring_copy(way, hop, order).wait_send()
    for zz in range(ZS):
        for which in range(2):
            sib_copy(zz, which).wait_send()
    for copy in total_copies():
        copy.wait_send()

    @pl.when(stays)
    def _():
        for part in range(3):
            grad_copy(part).wait_send()

    @pl.when(moves)
    def _():
        for copy in swap_copies():
            copy.wait_send()
        loss_copy.wait_send()
        for part in range(3):
            ret_copy(part).wait_send()
        for piece in range(PEERS):
            @pl.when(piece != peer)
            def _():
                rs_copy(piece).wait_send()
            fin_copy(piece).wait_send()
        for d in range(1, PEERS):
            ag_copy(d).wait_send()


def on_device(clip_embed, seg_feats, pair_index):
    bf16, f32, i32 = jnp.bfloat16, jnp.float32, jnp.int32
    vmem = pl.BlockSpec(memory_space=pltpu.VMEM)
    dma = pltpu.SemaphoreType.DMA
    return pl.pallas_call(
        kernel,
        name="ntxent",
        out_shape=(
            jax.ShapeDtypeStruct((1, ROWS), f32),
            jax.ShapeDtypeStruct((1, ROWS, E), f32),
            jax.ShapeDtypeStruct((ROWS, E), f32),
        ),
        in_specs=[vmem] * 3,
        out_specs=(vmem,) * 3,
        scratch_shapes=[
            pltpu.VMEM((ZS, PAIR, E), bf16),
            pltpu.VMEM((ZS, E, PAIR), bf16),
            pltpu.VMEM((ZS, PAIR, ROWS), bf16),
            pltpu.VMEM((ZS, 2, 1, ROWS), f32),
            pltpu.VMEM((E, ROWS), bf16),
            pltpu.VMEM((ROWS, E), bf16),
            pltpu.VMEM((ROWS, E), bf16),
            pltpu.VMEM((ROWS, E), bf16),
            pltpu.VMEM((1, ROWS), i32),
            pltpu.VMEM((1, ROWS), f32),
            pltpu.VMEM((E, ROWS), f32),
            pltpu.VMEM((E, ROWS), f32),
            pltpu.VMEM((E, ROWS), f32),
            pltpu.VMEM((E, ROWS), f32),
            pltpu.VMEM((ROWS, E), bf16),
            pltpu.VMEM((ROWS, E), bf16),
            pltpu.VMEM((ROWS, E), f32),
            pltpu.VMEM((1, ROWS), f32),
            pltpu.VMEM((1, ROWS), f32),
            pltpu.VMEM((ROWS, E), bf16),
            pltpu.VMEM((PEERS, PIECE, E), bf16),
            pltpu.VMEM((ROWS, E), bf16),
            dma((5,)), dma((5,)),
            dma((2, 7)), dma((2, 7)),
            dma((ZS, 2)), dma((ZS, 2)),
            dma((ZS, 2)), dma((ZS, 2)),
            dma((4,)), dma((4,)),
            dma((3,)), dma((3,)),
            dma((PEERS,)), dma((PEERS,)),
            dma((PEERS,)), dma((PEERS,)),
            dma((PEERS,)), dma((PEERS,)),
        ],
        compiler_params=pltpu.CompilerParams(
            collective_id=0, has_side_effects=True, vmem_limit_bytes=56 * 2**20
        ),
    )(clip_embed, seg_feats, pair_index)


def solution(mesh):
    placed = (P("clip", None), P("tm", "clip", None), P("tm", "clip"))
    return jax.shard_map(
        on_device,
        mesh=mesh,
        in_specs=placed,
        out_specs=(P("tm", "clip"), P("tm", "clip", None), P("clip", None)),
        check_vma=False,
    )
```

time: 589 us -> 81 us (0.14)
  waiting for transfers between devices: 295 us -> 0 us
  local copies, waits for them, and re-layouts: 127 us -> 4.24 us
  Pallas kernels: 0 us -> 75.9 us
  matrix products: 63.9 us -> 0 us
  other arithmetic: 58.7 us -> 0 us
  blocking collectives: 25.7 us -> 0 us
  between operations: 14.1 us -> 0.65 us
    psum x1 -> x0, waiting for transfers between devices: 151 us -> none  [on_device(): grad_clip = lax.psum(grad_seg, 'tm')]
    all_gather x1 -> x0, waiting for transfers between devices: 143 us -> none  [on_device(): shard_rows = lax.all_gather(unit, 'clip', axis=0, tiled=True)]
    gather x32 -> x0, local copies, waits for them, and re-layouts: 88.5 us -> none  [the longest x16 55.5 us: first_advance(): picked = jnp.take_along_axis(score, where_at[:, None], 1)[:, 0]]
    pallas_call x0 -> x1, Pallas kernels: none -> 75.9 us  [on_device(): pl.pallas_call(kernel, name='ntxent', out_shape=(jax.ShapeDtypeStruct((1,...]
    dot_general x48 -> x0, matrix products: 63.9 us -> none  [the longest x32 47.6 us: scores(): jnp.einsum('re,ce->rc', left_rows, right_rows, preferred_element_type=jnp...]
    add x64 -> x0, other arithmetic: 31.1 us -> none  [the longest x32 10.5 us: on_device(): own_rows = device * row_count + jnp.arange(row_count, dtype=jnp.int32)]
    all_gather x1 -> x0, blocking collectives: 25.7 us -> none  [on_device(): lax.all_gather(totals.astype(jnp.bfloat16), 'clip', axis=0, tiled=True)]
    dynamic_slice x32 -> x0, local copies, waits for them, and re-layouts: 19.2 us -> none  [on_device(): result, ignored = lax.scan(first_advance, start_pair, (stacked, offsets))]
  transfers between devices with their start and end apart: 2 -> 0, of which waited for: 2 -> 0; matrix products, arithmetic and copies ran while one was open for 0% -> 0% of each run, Pallas kernels for 0% -> 0%
where the time goes in v1:
time: 81 us; the launch traced here: 80.8 us
  Pallas kernels  75.9 us (94%)
  local copies, waits for them, and re-layouts  4.24 us (5%)
    pallas_call x1, Pallas kernels, on_device(): pl.pallas_call(kernel, name='ntxent', out_shape=(jax.ShapeDtypeStruct((1,...  75.9 us
    unnamed x7, local copies, waits for them, and re-layouts  4.24 us

profile of v1, /device:TPU:1, one launch (start us, length us, event | category | flops | bytes accessed | tf_op | source)
XLA Modules:
  0.0 80.8 jit_solution(14591124799661720197)
XLA Ops:
  0.6 75.9 %ntxent.1 = (f32[1,384]{1,0:T(1,128)}, f32[1,384,512]{2,1,0:T(8,128)}, f32[384,512]{1,0:T(8,128)}) custom-call(bf16[384,512]{1,0:T(8,128)(2,1)} %clip_ref.1, bf16[1,384,512]{2,1,0:T(8,128)(2,1)} %feat_ref.1, s32[1,384]{1,0:T(1,128)} %pair_ref.1), custom_call_target="tpu_custom_call" | custom-call | tf_op jit(solution)/shard_map/ntxent/pallas_call | solution.py:398
  76.6 0.0 copy-start.1
  76.6 0.7 copy-done.1
  77.2 0.6 copy.9
  77.8 0.0 copy-start
  77.8 2.1 %copy.10 = f32[1,384,512]{2,1,0:T(8,128)} copy(f32[1,384,512]{2,1,0:T(8,128)} %get-tuple-element.7) | data formatting | bytes 1572864
  79.9 0.0 copy-done
  79.9 0.9 %copy.11 = f32[384,512]{1,0:T(8,128)} copy(f32[384,512]{1,0:T(8,128)S(1)} %copy-done) | data formatting | bytes 1572864
Async XLA Ops:
  76.6 0.7 copy-start.1
  77.8 2.1 %copy-start = (f32[384,512]{1,0:T(8,128)S(1)}, f32[384,512]{1,0:T(8,128)}, u32[]{:S(2)}) copy-start(f32[384,512]{1,0:T(8,128)} %get-tuple-element.8) | copy-start | bytes 2359300

commit v2 on v1

v2 whole, which is shorter than its diff:
```python
import math

import jax
import jax.numpy as jnp
from jax import lax
from jax.experimental import pallas as pl
from jax.experimental.pallas import tpu as pltpu
from jax.sharding import PartitionSpec as P

MESH = pl.DeviceIdType.MESH
logit_scale = 14.0
norm_eps = 1e-06
exp2_scale = logit_scale * math.log2(math.e)

RS_DTYPE = jnp.bfloat16
ZS = 8
ROWS = 384
CHUNKS = 4
CHUNK = ROWS // CHUNKS
PAIR = 2 * ROWS
E = 512
PEERS = 8
PARTS = 3
PART = ROWS // PARTS
PIECE = PART // PEERS
RING_COPIES = CHUNKS * 7 // 2


def remote(src, dst, send_sem, recv_sem, device):
    return pltpu.make_async_remote_copy(
        src_ref=src, dst_ref=dst, send_sem=send_sem, recv_sem=recv_sem,
        device_id=device, device_id_type=MESH,
    )


def dot(a, b):
    return jnp.dot(a, b, preferred_element_type=jnp.float32)


def kernel(
    clip_hbm, feat_hbm, pair_hbm,
    loss_out, seg_out, gathered,
    u_all, ut_all, expo_all, columns, tot_all, unit_t, stage, raw_clip, raw_feat, home_clip, home_feat, partner, totals,
    pull_one, pull_pos, acc, summed_t, ret_stage, ret, sib_grad, loss_stage, loss_ret,
    rs_send, rs_buf,
    load_s, swap_s, swap_r, ring_s, ring_r, sib_s, sib_r, tot_s, tot_r, ret_s, ret_r, grad_s, grad_r,
    rs_s, rs_r, ag_s, ag_r, fin_s, fin_r,
):
    clip = lax.axis_index("clip")
    tm = lax.axis_index("tm")
    z, x = clip // 2, lax.rem(clip, 2)
    peer, core = tm // 2, lax.rem(tm, 2)
    stays = x == core
    moves = x != core

    def at(zz, xx, pp, cc):
        return (zz * 2 + xx, pp * 2 + cc)

    def ring(offset):
        return lax.rem(z + offset + ZS, ZS)

    sibling = at(z, x, peer, 1 - core)
    swapped = at(z, 1 - x, peer, 1 - core)

    barrier = pltpu.get_barrier_semaphore()

    def greet(device):
        pl.semaphore_signal(barrier, inc=1, device_id=device, device_id_type=MESH)

    greet(at(ring(1), x, peer, core))
    greet(at(ring(-1), x, peer, core))
    greet(sibling)

    @pl.when(moves)
    def _():
        greet(swapped)
        for d in range(1, PEERS):
            greet(at(z, x, lax.rem(peer + d, PEERS), core))

    loads = [
        pltpu.make_async_copy(clip_hbm, home_clip, load_s.at[0]),
        pltpu.make_async_copy(feat_hbm.at[0], home_feat, load_s.at[1]),
    ]
    pair_load = pltpu.make_async_copy(pair_hbm, partner, load_s.at[2])
    for load in loads:
        load.start()
    for load in loads:
        load.wait()

    summed = home_clip[...].astype(jnp.float32) + home_feat[...].astype(jnp.float32)
    factor = lax.rsqrt(jnp.sum(summed * summed, 1, keepdims=True) + E * norm_eps)
    unit = (summed * factor).astype(jnp.bfloat16)

    def chunk_of(zz, block, which):
        return u_all.at[zz, pl.ds(pl.multiple_of(block * ROWS + which * CHUNK, CHUNK), CHUNK)]

    def swap_unit(which, block):
        return remote(stage.at[pl.ds(which * CHUNK, CHUNK)], chunk_of(z, block, which),
                      swap_s.at[which], swap_r.at[which], swapped)

    def swap_raw():
        return [
            remote(feat_hbm.at[0], raw_feat, swap_s.at[CHUNKS], swap_r.at[CHUNKS], swapped),
            remote(clip_hbm, raw_clip, swap_s.at[CHUNKS + 1], swap_r.at[CHUNKS + 1], swapped),
        ]

    swap_pair = remote(pair_hbm, partner, swap_s.at[CHUNKS + 2], swap_r.at[CHUNKS + 2], swapped)

    def order_chunk(way, order):
        return order if way == 0 else CHUNKS - 1 - order

    def ring_copy(way, hop, order):
        source, target = (ring(-hop), ring(1)) if way == 0 else (ring(hop), ring(-1))
        ref = chunk_of(source, core, order_chunk(way, order))
        index = CHUNKS * hop + order
        return remote(ref, ref, ring_s.at[way, index], ring_r.at[way, index], at(target, x, peer, core))

    def sib_copy(source, which):
        ref = chunk_of(source, core, which)
        return remote(ref, ref, sib_s.at[source, which], sib_r.at[source, which], sibling)

    def sib_arrival(source, which):
        ref = chunk_of(source, 1 - core, which)
        return remote(ref, ref, sib_s.at[source, which], sib_r.at[source, which], sibling)

    swap_order = [c for o in range(CHUNKS // 2) for c in (o, CHUNKS - 1 - o)]

    @pl.when(stays)
    def _():
        pair_load.start()
        u_all[z, pl.ds(pl.multiple_of(core * ROWS, ROWS), ROWS), :] = unit
        pl.semaphore_wait(barrier, 3)
        for order in range(CHUNKS):
            for way in range(2):
                ring_copy(way, 0, order).start()
        for which in swap_order:
            sib_copy(z, which).start()
        raw_clip[...] = home_clip[...]
        raw_feat[...] = home_feat[...]
        pair_load.wait()

    @pl.when(moves)
    def _():
        stage[...] = unit
        pl.semaphore_wait(barrier, 3 + PEERS)
        for which in swap_order:
            swap_unit(which, x).start()
        swap_pair.start()
        for order in range(CHUNKS // 2):
            for which in (order, CHUNKS - 1 - order):
                swap_unit(which, core).wait_recv()
            for way in range(2):
                ring_copy(way, 0, order).start()
            for which in (order, CHUNKS - 1 - order):
                sib_copy(z, which).start()
        for order in range(CHUNKS // 2, CHUNKS):
            for way in range(2):
                ring_copy(way, 0, order).start()
        swap_pair.wait_recv()

    unit_t[...] = u_all[z, pl.ds(pl.multiple_of(core * ROWS, ROWS), ROWS), :].T
    totals[...] = jnp.zeros_like(totals)
    pull_one[...] = jnp.zeros_like(pull_one)
    pull_pos[...] = jnp.zeros_like(pull_pos)

    def column_ids(zz):
        return lax.broadcasted_iota(jnp.int32, (PAIR, ROWS), 0) + zz * PAIR

    def block_of(step):
        hop = (step + 1) // 2
        return ring(jnp.where(lax.rem(step, 2) == 1, -hop, hop))

    def score_part(zz):
        score = dot(u_all[zz], unit_t[...])
        own = lax.broadcasted_iota(jnp.int32, (1, ROWS), 1) + (z * PAIR + core * ROWS)
        expo = jnp.where(column_ids(zz) != own, jnp.exp2(score * exp2_scale - exp2_scale), 0.0)
        totals[...] += jnp.sum(expo, 0, keepdims=True)
        expo_all[zz] = expo.astype(jnp.bfloat16)

    def pull_part(zz):
        ut_all[zz] = u_all[zz].T
        columns[:, :ROWS] = expo_all[zz]
        columns[:, ROWS:] = jnp.where(column_ids(zz) == partner[...], 1.0, 0.0).astype(jnp.bfloat16)
        both = dot(ut_all[zz], columns[...])
        pull_one[...] += both[:, :ROWS]
        pull_pos[...] += both[:, ROWS:]

    def send_on(way, hop, order):
        @pl.when(hop <= (3 if order < CHUNKS // 2 else 2))
        def _():
            ring_copy(way, hop, order).start()

        source = ring(-hop) if way == 0 else ring(hop)
        sib_copy(source, order_chunk(way, order)).start()

    def pass_on(hop, order):
        for way in range(2):
            source = ring(-hop) if way == 0 else ring(hop)
            ref = chunk_of(source, core, order_chunk(way, order))
            index = CHUNKS * (hop - 1) + order
            remote(ref, ref, ring_s.at[way, index], ring_r.at[way, index], sibling).wait_recv()
            send_on(way, hop, order)

    def events(k, part):
        hop = k // 2 + 1
        group = CHUNKS // 4
        for odd in range(2):
            orders = [odd * (CHUNKS // 2) + part * group + i for i in range(group)]

            @pl.when(lax.rem(k, 2) == odd)
            def _():
                for order in orders:
                    pass_on(hop, order)

    def gather_step(step, carry):
        @pl.when(step < 6)
        def _():
            events(step, 0)

        @pl.when(step > 0)
        def _():
            pull_part(block_of(step - 1))

        @pl.when(step < 6)
        def _():
            events(step, 1)

        @pl.when((step == 3) & moves)
        def _():
            for copy in swap_raw():
                copy.start()

        @pl.when(step == 6)
        def _():
            @pl.when(moves)
            def _():
                for copy in swap_raw():
                    copy.wait_recv()

            summed_t[...] = (raw_clip[...].astype(jnp.float32) + raw_feat[...].astype(jnp.float32)).T

        @pl.when(step == 7)
        def _():
            events(step - 1, 0)
            events(step - 1, 1)

        zz = block_of(step)
        for which in range(CHUNKS):
            sib_arrival(zz, which).wait_recv()
        score_part(zz)
        return carry

    lax.fori_loop(0, ZS, gather_step, 0)

    tot_all[z, core] = totals[...]
    others = [(dz, dc) for dz in (4, 3, 5, 2, 6, 1, 7, 0) for dc in range(2) if dz or dc]

    def total_copy(dz, dc):
        ref = tot_all.at[z, core]
        return remote(ref, ref, tot_s.at[dz, dc], tot_r.at[z, core], at(ring(dz), x, peer, lax.rem(core + dc, 2)))

    def total_arrival(zz, block):
        ref = tot_all.at[zz, block]
        return remote(ref, ref, tot_s.at[0, 0], tot_r.at[zz, block], sibling)

    loss_copy = remote(loss_stage, loss_ret, ret_s.at[PARTS], ret_r.at[PARTS], swapped)

    for dz, dc in others:
        total_copy(dz, dc).start()
    pull_part(block_of(ZS - 1))

    inverse = 1.0 / totals[...]
    positive = jnp.sum(unit_t[...].astype(jnp.float32) * pull_pos[...], 0, keepdims=True)
    loss = logit_scale * (1.0 - positive) + jnp.log(totals[...])

    @pl.when(stays)
    def _():
        loss_out[...] = loss

    @pl.when(moves)
    def _():
        loss_stage[...] = loss
        loss_copy.start()
    acc[...] = inverse * pull_one[...] - 2.0 * pull_pos[...]
    factor_t = lax.rsqrt(jnp.sum(summed_t[...] * summed_t[...], 0, keepdims=True) + E * norm_eps)

    def second(zz, own):
        if not own:
            total_arrival(zz, core).wait_recv()
        total_arrival(zz, 1 - core).wait_recv()
        scale = 1.0 / jnp.concatenate([tot_all[zz, 0], tot_all[zz, 1]], 1)
        scaled = (ut_all[zz].astype(jnp.float32) * scale).astype(jnp.bfloat16)
        return dot(scaled, expo_all[zz])

    def second_hop(hop, carry):
        acc[...] += second(ring(-hop), False) + second(ring(hop), False)
        return carry

    acc[...] += second(z, True)
    lax.fori_loop(1, 4, second_hop, 0)
    acc[...] += second(ring(4), False)

    def part_rows(part):
        return slice(part * PART, (part + 1) * PART)

    def ret_copy(part):
        rows = pl.ds(part * PART, PART)
        return remote(ret_stage.at[rows], ret.at[rows], ret_s.at[part], ret_r.at[part], swapped)

    def grad_copy(part):
        rows = pl.ds(part * PART, PART)
        return remote(seg_out.at[0, rows], sib_grad.at[rows], grad_s.at[part], grad_r.at[part], sibling)

    for part in range(PARTS):
        rows = part_rows(part)
        grad_unit = logit_scale * acc[:, rows]
        summed_part = summed_t[:, rows]
        factor_part = factor_t[:, rows]
        along = jnp.sum(summed_part * grad_unit, 0, keepdims=True)
        grad = (factor_part * grad_unit - factor_part**3 * along * summed_part).T

        @pl.when(stays)
        def _():
            seg_out[0, rows, :] = grad
            grad_copy(part).start()

        @pl.when(moves)
        def _():
            ret_stage[rows, :] = grad.astype(jnp.bfloat16)
            ret_copy(part).start()

    def rs_copy(part, d):
        owner = lax.rem(peer + d, PEERS)
        rows = pl.ds(pl.multiple_of(part * PART + owner * PIECE, PIECE), PIECE)
        return remote(rs_send.at[rows], rs_buf.at[part, peer], rs_s.at[part, d], rs_r.at[part, peer],
                      at(z, x, owner, core))

    def rs_arrival(part, d):
        source = lax.rem(peer + d, PEERS)
        ref = rs_buf.at[part, source]
        return remote(ref, ref, rs_s.at[part, d], rs_r.at[part, source], sibling)

    def gathered_rows(part, owner):
        return gathered.at[pl.ds(pl.multiple_of(part * PART + owner * PIECE, PIECE), PIECE)]

    def ag_copy(part, d):
        ref = gathered_rows(part, peer)
        return remote(ref, ref, ag_s.at[part, d], ag_r.at[part, peer], at(z, x, lax.rem(peer + d, PEERS), core))

    def ag_arrival(part, source):
        ref = gathered_rows(part, source)
        return remote(ref, ref, ag_s.at[part, 0], ag_r.at[part, source], sibling)

    def fin_copy(part):
        ref = gathered.at[pl.ds(part * PART, PART)]
        return remote(ref, ref, fin_s.at[part], fin_r.at[part], sibling)

    @pl.when(moves)
    def _():
        loss_copy.wait_recv()
        loss_out[...] = loss_ret[...]
        for part in range(PARTS):
            rows = part_rows(part)
            ret_copy(part).wait_recv()
            grad_copy(part).wait_recv()
            home = ret[rows, :].astype(jnp.float32)
            seg_out[0, rows, :] = home
            rs_send[rows, :] = (home + sib_grad[rows, :]).astype(RS_DTYPE)
            for d in (4, 3, 5, 2, 6, 1, 7):
                rs_copy(part, d).start()
            rs_buf[part, peer] = rs_send[pl.ds(pl.multiple_of(part * PART + peer * PIECE, PIECE), PIECE), :]
        for part in range(PARTS):
            for d in range(1, PEERS):
                rs_arrival(part, d).wait_recv()
            reduced = rs_buf[part, 0].astype(jnp.float32)
            for source in range(1, PEERS):
                reduced += rs_buf[part, source].astype(jnp.float32)
            gathered[pl.ds(pl.multiple_of(part * PART + peer * PIECE, PIECE), PIECE), :] = reduced.astype(jnp.bfloat16)
            for d in (4, 3, 5, 2, 6, 1, 7):
                ag_copy(part, d).start()
        for part in range(PARTS):
            for d in (1, 7, 2, 6, 3, 5, 4):
                source = lax.rem(peer + PEERS - d, PEERS)
                ag_arrival(part, source).wait_recv()
            fin_copy(part).start()

    @pl.when(stays)
    def _():
        for part in range(PARTS):
            fin_copy(part).wait_recv()

    for way in range(2):
        for index in range(RING_COPIES):
            ring_copy(way, index // CHUNKS, index % CHUNKS).wait_send()
    for zz in range(ZS):
        for which in range(CHUNKS):
            sib_copy(zz, which).wait_send()
    for dz, dc in others:
        total_copy(dz, dc).wait_send()

    @pl.when(stays)
    def _():
        for part in range(PARTS):
            grad_copy(part).wait_send()

    @pl.when(moves)
    def _():
        for which in range(CHUNKS):
            swap_unit(which, x).wait_send()
        swap_pair.wait_send()
        for copy in swap_raw():
            copy.wait_send()
        loss_copy.wait_send()
        for part in range(PARTS):
            ret_copy(part).wait_send()
            for d in range(1, PEERS):
                rs_copy(part, d).wait_send()
            for d in range(1, PEERS):
                ag_copy(part, d).wait_send()
            fin_copy(part).wait_send()


def hand_over(loss_in, seg_in, sum_in, loss_out, seg_out, clip_out, wide, sems):
    copies = [
        pltpu.make_async_copy(seg_in, seg_out, sems.at[0]),
        pltpu.make_async_copy(loss_in, loss_out, sems.at[1]),
        pltpu.make_async_copy(wide, clip_out, sems.at[2]),
    ]
    for copy in copies[:2]:
        copy.start()
    wide[...] = sum_in[...].astype(jnp.float32)
    copies[2].start()
    for copy in copies:
        copy.wait()


def on_device(clip_embed, seg_feats, pair_index):
    bf16, f32, i32 = jnp.bfloat16, jnp.float32, jnp.int32
    vmem = pl.BlockSpec(memory_space=pltpu.VMEM)
    anywhere = pl.BlockSpec(memory_space=pl.ANY)
    hbm = pl.BlockSpec(memory_space=pltpu.HBM)
    dma = pltpu.SemaphoreType.DMA
    loss, seg, total = pl.pallas_call(
        kernel,
        name="ntxent",
        out_shape=(
            pltpu.VMEM((1, ROWS), f32),
            pltpu.VMEM((1, ROWS, E), f32),
            pltpu.VMEM((ROWS, E), bf16),
        ),
        in_specs=[hbm] * 3,
        out_specs=(vmem,) * 3,
        scratch_shapes=[
            pltpu.VMEM((ZS, PAIR, E), bf16),
            pltpu.VMEM((ZS, E, PAIR), bf16),
            pltpu.VMEM((ZS, PAIR, ROWS), bf16),
            pltpu.VMEM((PAIR, 2 * ROWS), bf16),
            pltpu.VMEM((ZS, 2, 1, ROWS), f32),
            pltpu.VMEM((E, ROWS), bf16),
            pltpu.VMEM((ROWS, E), bf16),
            pltpu.VMEM((ROWS, E), bf16),
            pltpu.VMEM((ROWS, E), bf16),
            pltpu.VMEM((ROWS, E), bf16),
            pltpu.VMEM((ROWS, E), bf16),
            pltpu.VMEM((1, ROWS), i32),
            pltpu.VMEM((1, ROWS), f32),
            pltpu.VMEM((E, ROWS), f32),
            pltpu.VMEM((E, ROWS), f32),
            pltpu.VMEM((E, ROWS), f32),
            pltpu.VMEM((E, ROWS), f32),
            pltpu.VMEM((ROWS, E), bf16),
            pltpu.VMEM((ROWS, E), bf16),
            pltpu.VMEM((ROWS, E), f32),
            pltpu.VMEM((1, ROWS), f32),
            pltpu.VMEM((1, ROWS), f32),
            pltpu.VMEM((ROWS, E), RS_DTYPE),
            pltpu.VMEM((PARTS, PEERS, PIECE, E), RS_DTYPE),
            dma((3,)),
            dma((CHUNKS + 3,)), dma((CHUNKS + 3,)),
            dma((2, RING_COPIES)), dma((2, RING_COPIES)),
            dma((ZS, CHUNKS)), dma((ZS, CHUNKS)),
            dma((ZS, 2)), dma((ZS, 2)),
            dma((PARTS + 1,)), dma((PARTS + 1,)),
            dma((PARTS,)), dma((PARTS,)),
            dma((PARTS, PEERS)), dma((PARTS, PEERS)),
            dma((PARTS, PEERS)), dma((PARTS, PEERS)),
            dma((PARTS,)), dma((PARTS,)),
        ],
        compiler_params=pltpu.CompilerParams(
            collective_id=0, has_side_effects=True, vmem_limit_bytes=56 * 2**20
        ),
    )(clip_embed, seg_feats, pair_index)
    return pl.pallas_call(
        hand_over,
        name="hand_over",
        out_shape=(
            jax.ShapeDtypeStruct((1, ROWS), f32),
            jax.ShapeDtypeStruct((1, ROWS, E), f32),
            jax.ShapeDtypeStruct((ROWS, E), f32),
        ),
        in_specs=[vmem] * 3,
        out_specs=(anywhere,) * 3,
        scratch_shapes=[pltpu.VMEM((ROWS, E), f32), dma((3,))],
        compiler_params=pltpu.CompilerParams(vmem_limit_bytes=4 * 2**20),
    )(loss, seg, total)


def solution(mesh):
    placed = (P("clip", None), P("tm", "clip", None), P("tm", "clip"))
    return jax.shard_map(
        on_device,
        mesh=mesh,
        in_specs=placed,
        out_specs=(P("tm", "clip"), P("tm", "clip", None), P("clip", None)),
        check_vma=False,
    )
```

time: 81 us -> 74.1 us (0.915)
  local copies, waits for them, and re-layouts: 4.24 us -> 0 us
  Pallas kernels: 75.9 us -> 72.5 us
    unnamed x7 -> x0, local copies, waits for them, and re-layouts: 4.24 us -> none
    pallas_call x1 -> x2, Pallas kernels: 75.9 us -> 72.5 us  [the longest x1 71.3 us: on_device(): pl.pallas_call(kernel, name='ntxent', out_shape=(pltpu.VMEM((1, ROWS), f3...]
where the time goes in v2:
time: 74.1 us; the launch traced here: 73.1 us
  Pallas kernels  72.5 us (98%)
    pallas_call x1, Pallas kernels, on_device(): pl.pallas_call(kernel, name='ntxent', out_shape=(pltpu.VMEM((1, ROWS), f3...  71.3 us

profile of v2, /device:TPU:1, one launch (start us, length us, event | category | flops | bytes accessed | tf_op | source)
XLA Modules:
  0.0 73.1 jit_solution(7727990588276596125)
XLA Ops:
  0.6 71.3 %ntxent.1 = (f32[1,384]{1,0:T(1,128)S(1)}, f32[1,384,512]{2,1,0:T(8,128)S(1)}, bf16[384,512]{1,0:T(8,128)(2,1)S(1)}) custom-call(bf16[384,512]{1,0:T(8,128)(2,1)} %clip_hbm.1, bf16[1,384,512]{2,1,0:T(8,128)(2,1)} %feat_hbm.1, s32[1,384]{1,0:T(1,128)} %pair_hbm.1), custom_call_target="tpu_custom_call" | custom-call | tf_op jit(solution)/shard_map/ntxent/pallas_call | solution.py:443
  71.9 1.2 %hand_over.1 = (f32[1,384]{1,0:T(1,128)}, f32[1,384,512]{2,1,0:T(8,128)}, f32[384,512]{1,0:T(8,128)}) custom-call(f32[1,384]{1,0:T(1,128)S(1)} %get-tuple-element.6.loss_in, f32[1,384,512]{2,1,0:T(8,128)S(1)} %get-tuple-element.7.seg_in, bf16[384,512]{1,0:T(8,128)(2,1)S(1)} %get-tuple-element.8.sum_in), custom_call_target="tpu_custom_call" | custom-call | tf_op jit(solution)/shard_map/hand_over/pallas_call | solution.py:493

commit v3 on v2

--- a/solution.py
+++ b/solution.py
@@ -44,7 +44,7 @@
     pull_one, pull_pos, acc, summed_t, ret_stage, ret, sib_grad, loss_stage, loss_ret,
     rs_send, rs_buf,
     load_s, swap_s, swap_r, ring_s, ring_r, sib_s, sib_r, tot_s, tot_r, ret_s, ret_r, grad_s, grad_r,
-    rs_s, rs_r, ag_s, ag_r, fin_s, fin_r,
+    rs_s, rs_r, ag_s, ag_r, fin_s, fin_r, near, go,
 ):
     clip = lax.axis_index("clip")
     tm = lax.axis_index("tm")
@@ -64,18 +64,21 @@
 
     barrier = pltpu.get_barrier_semaphore()
 
-    def greet(device):
-        pl.semaphore_signal(barrier, inc=1, device_id=device, device_id_type=MESH)
-
-    greet(at(ring(1), x, peer, core))
-    greet(at(ring(-1), x, peer, core))
-    greet(sibling)
+    def greet(device, semaphore):
+        pl.semaphore_signal(semaphore, inc=1, device_id=device, device_id_type=MESH)
+
+    neighbours = [at(ring(1), x, peer, core), at(ring(-1), x, peer, core), swapped]
+
+    @pl.when(stays)
+    def _():
+        for device in neighbours:
+            greet(device, barrier)
 
     @pl.when(moves)
     def _():
-        greet(swapped)
+        greet(sibling, barrier)
         for d in range(1, PEERS):
-            greet(at(z, x, lax.rem(peer + d, PEERS), core))
+            greet(at(z, x, lax.rem(peer + d, PEERS), core), barrier)
 
     loads = [
         pltpu.make_async_copy(clip_hbm, home_clip, load_s.at[0]),
@@ -129,12 +132,16 @@
     def _():
         pair_load.start()
         u_all[z, pl.ds(pl.multiple_of(core * ROWS, ROWS), ROWS), :] = unit
-        pl.semaphore_wait(barrier, 3)
+        pl.semaphore_wait(barrier, 4)
+        for device in neighbours:
+            greet(device, near)
         for order in range(CHUNKS):
             for way in range(2):
                 ring_copy(way, 0, order).start()
         for which in swap_order:
             sib_copy(z, which).start()
+        pl.semaphore_wait(near, 3)
+        greet(sibling, go)
         raw_clip[...] = home_clip[...]
         raw_feat[...] = home_feat[...]
         pair_load.wait()
@@ -142,7 +149,7 @@
     @pl.when(moves)
     def _():
         stage[...] = unit
-        pl.semaphore_wait(barrier, 3 + PEERS)
+        pl.semaphore_wait(go, 1)
         for which in swap_order:
             swap_unit(which, x).start()
         swap_pair.start()
@@ -213,17 +220,19 @@
                     pass_on(hop, order)
 
     def gather_step(step, carry):
-        @pl.when(step < 6)
-        def _():
-            events(step, 0)
+        group = jnp.minimum(step, 6)
+
+        @pl.when(step != 6)
+        def _():
+            events(group, 0)
 
         @pl.when(step > 0)
         def _():
             pull_part(block_of(step - 1))
 
-        @pl.when(step < 6)
-        def _():
-            events(step, 1)
+        @pl.when(step != 6)
+        def _():
+            events(group, 1)
 
         @pl.when((step == 3) & moves)
         def _():
@@ -238,11 +247,6 @@
                     copy.wait_recv()
 
             summed_t[...] = (raw_clip[...].astype(jnp.float32) + raw_feat[...].astype(jnp.float32)).T
-
-        @pl.when(step == 7)
-        def _():
-            events(step - 1, 0)
-            events(step - 1, 1)
 
         zz = block_of(step)
         for which in range(CHUNKS):
@@ -357,6 +361,7 @@
 
     @pl.when(moves)
     def _():
+        pl.semaphore_wait(barrier, PEERS - 1)
         loss_copy.wait_recv()
         loss_out[...] = loss_ret[...]
         for part in range(PARTS):
@@ -485,6 +490,7 @@
             dma((PARTS, PEERS)), dma((PARTS, PEERS)),
             dma((PARTS, PEERS)), dma((PARTS, PEERS)),
             dma((PARTS,)), dma((PARTS,)),
+            pltpu.SemaphoreType.REGULAR, pltpu.SemaphoreType.REGULAR,
         ],
         compiler_params=pltpu.CompilerParams(
             collective_id=0, has_side_effects=True, vmem_limit_bytes=56 * 2**20

time: 74.1 us -> 72.6 us (0.980); the launches traced: 73.1 us -> 72.4 us
  no operation moved by 1% of the time
where the time goes in v3:
time: 72.6 us; the launch traced here: 72.4 us
  Pallas kernels  71.8 us (99%)
    pallas_call x1, Pallas kernels, on_device(): pl.pallas_call(kernel, name='ntxent', out_shape=(pltpu.VMEM((1, ROWS), f3...  70.6 us

profile of v3, /device:TPU:1, one launch (start us, length us, event | category | flops | bytes accessed | tf_op | source)
XLA Modules:
  0.0 72.4 jit_solution(15928727000322088988)
XLA Ops:
  0.6 70.6 %ntxent.1 = (f32[1,384]{1,0:T(1,128)S(1)}, f32[1,384,512]{2,1,0:T(8,128)S(1)}, bf16[384,512]{1,0:T(8,128)(2,1)S(1)}) custom-call(bf16[384,512]{1,0:T(8,128)(2,1)} %clip_hbm.1, bf16[1,384,512]{2,1,0:T(8,128)(2,1)} %feat_hbm.1, s32[1,384]{1,0:T(1,128)} %pair_hbm.1), custom_call_target="tpu_custom_call" | custom-call | tf_op jit(solution)/shard_map/ntxent/pallas_call | solution.py:448
  71.2 1.2 %hand_over.1 = (f32[1,384]{1,0:T(1,128)}, f32[1,384,512]{2,1,0:T(8,128)}, f32[384,512]{1,0:T(8,128)}) custom-call(f32[1,384]{1,0:T(1,128)S(1)} %get-tuple-element.6.loss_in, f32[1,384,512]{2,1,0:T(8,128)S(1)} %get-tuple-element.7.seg_in, bf16[384,512]{1,0:T(8,128)(2,1)S(1)} %get-tuple-element.8.sum_in), custom_call_target="tpu_custom_call" | custom-call | tf_op jit(solution)/shard_map/hand_over/pallas_call | solution.py:499

commit v4 on v3

--- a/solution.py
+++ b/solution.py
@@ -12,7 +12,6 @@
 norm_eps = 1e-06
 exp2_scale = logit_scale * math.log2(math.e)
 
-RS_DTYPE = jnp.bfloat16
 ZS = 8
 ROWS = 384
 CHUNKS = 4
@@ -40,11 +39,11 @@
 def kernel(
     clip_hbm, feat_hbm, pair_hbm,
     loss_out, seg_out, gathered,
-    u_all, ut_all, expo_all, columns, tot_all, unit_t, stage, raw_clip, raw_feat, home_clip, home_feat, partner, totals,
-    pull_one, pull_pos, acc, summed_t, ret_stage, ret, sib_grad, loss_stage, loss_ret,
-    rs_send, rs_buf,
-    load_s, swap_s, swap_r, ring_s, ring_r, sib_s, sib_r, tot_s, tot_r, ret_s, ret_r, grad_s, grad_r,
-    rs_s, rs_r, ag_s, ag_r, fin_s, fin_r, near, go,
+    u_all, ut_all, expo_all, columns, scaled_last, tot_all, unit_t, stage, raw_clip, raw_feat, home_clip, home_feat, partner, totals,
+    pull_one, pull_pos, acc, summed_t, ret_stage, ret, loss_stage, loss_ret,
+    rs_buf,
+    load_s, swap_s, swap_r, ring_s, ring_r, sib_s, sib_r, tot_s, tot_r, ret_s, ret_r,
+    rs_s, rs_r, ag_s, ag_r, fin_s, fin_r, near, go, peers_in,
 ):
     clip = lax.axis_index("clip")
     tm = lax.axis_index("tm")
@@ -73,12 +72,12 @@
     def _():
         for device in neighbours:
             greet(device, barrier)
+        for d in range(PEERS):
+            greet(at(z, 1 - x, lax.rem(peer + d, PEERS), core), barrier)
 
     @pl.when(moves)
     def _():
         greet(sibling, barrier)
-        for d in range(1, PEERS):
-            greet(at(z, x, lax.rem(peer + d, PEERS), core), barrier)
 
     loads = [
         pltpu.make_async_copy(clip_hbm, home_clip, load_s.at[0]),
@@ -273,6 +272,12 @@
         total_copy(dz, dc).start()
     pull_part(block_of(ZS - 1))
 
+    @pl.when(moves)
+    def _():
+        pl.semaphore_wait(barrier, PEERS)
+        greet(at(z, 1 - x, peer, core), peers_in)
+
+
     inverse = 1.0 / totals[...]
     positive = jnp.sum(unit_t[...].astype(jnp.float32) * pull_pos[...], 0, keepdims=True)
     loss = logit_scale * (1.0 - positive) + jnp.log(totals[...])
@@ -302,7 +307,11 @@
 
     acc[...] += second(z, True)
     lax.fori_loop(1, 4, second_hop, 0)
-    acc[...] += second(ring(4), False)
+    last = ring(4)
+    total_arrival(last, core).wait_recv()
+    total_arrival(last, 1 - core).wait_recv()
+    scale = 1.0 / jnp.concatenate([tot_all[last, 0], tot_all[last, 1]], 1)
+    scaled_last[...] = (ut_all[last].astype(jnp.float32) * scale).astype(jnp.bfloat16)
 
     def part_rows(part):
         return slice(part * PART, (part + 1) * PART)
@@ -311,13 +320,30 @@
         rows = pl.ds(part * PART, PART)
         return remote(ret_stage.at[rows], ret.at[rows], ret_s.at[part], ret_r.at[part], swapped)
 
-    def grad_copy(part):
-        rows = pl.ds(part * PART, PART)
-        return remote(seg_out.at[0, rows], sib_grad.at[rows], grad_s.at[part], grad_r.at[part], sibling)
+    def piece_rows(part, owner):
+        return pl.ds(pl.multiple_of(part * PART + owner * PIECE, PIECE), PIECE)
+
+    def rs_copy(part, d, crosses):
+        owner = lax.rem(peer + d, PEERS)
+        source = peer + PEERS if crosses else peer
+        return remote(ret_stage.at[piece_rows(part, owner)], rs_buf.at[part, source], rs_s.at[part, d], rs_r.at[part, source],
+                      at(z, 1 - x if crosses else x, owner, core))
+
+    def rs_arrival(part, source):
+        ref = rs_buf.at[part, source]
+        return remote(ref, ref, rs_s.at[part, 0], rs_r.at[part, source], sibling)
+
+    far_first = (4, 3, 5, 2, 6, 1, 7)
+
+    @pl.when(stays)
+    def _():
+        pl.semaphore_wait(peers_in, 1)
 
     for part in range(PARTS):
         rows = part_rows(part)
-        grad_unit = logit_scale * acc[:, rows]
+        field = acc[:, rows]
+        field += dot(scaled_last[...], expo_all[ring(4), :, rows])
+        grad_unit = logit_scale * field
         summed_part = summed_t[:, rows]
         factor_part = factor_t[:, rows]
         along = jnp.sum(summed_part * grad_unit, 0, keepdims=True)
@@ -325,74 +351,22 @@
 
         @pl.when(stays)
         def _():
+            ret_stage[rows, :] = grad.astype(jnp.bfloat16)
+            for d in far_first:
+                rs_copy(part, d, False).start()
             seg_out[0, rows, :] = grad
-            grad_copy(part).start()
+            rs_buf[part, peer] = ret_stage[piece_rows(part, peer), :]
 
         @pl.when(moves)
         def _():
             ret_stage[rows, :] = grad.astype(jnp.bfloat16)
+            for d in far_first + (0,):
+                rs_copy(part, d, True).start()
+
+    @pl.when(moves)
+    def _():
+        for part in range(PARTS):
             ret_copy(part).start()
-
-    def rs_copy(part, d):
-        owner = lax.rem(peer + d, PEERS)
-        rows = pl.ds(pl.multiple_of(part * PART + owner * PIECE, PIECE), PIECE)
-        return remote(rs_send.at[rows], rs_buf.at[part, peer], rs_s.at[part, d], rs_r.at[part, peer],
-                      at(z, x, owner, core))
-
-    def rs_arrival(part, d):
-        source = lax.rem(peer + d, PEERS)
-        ref = rs_buf.at[part, source]
-        return remote(ref, ref, rs_s.at[part, d], rs_r.at[part, source], sibling)
-
-    def gathered_rows(part, owner):
-        return gathered.at[pl.ds(pl.multiple_of(part * PART + owner * PIECE, PIECE), PIECE)]
-
-    def ag_copy(part, d):
-        ref = gathered_rows(part, peer)
-        return remote(ref, ref, ag_s.at[part, d], ag_r.at[part, peer], at(z, x, lax.rem(peer + d, PEERS), core))
-
-    def ag_arrival(part, source):
-        ref = gathered_rows(part, source)
-        return remote(ref, ref, ag_s.at[part, 0], ag_r.at[part, source], sibling)
-
-    def fin_copy(part):
-        ref = gathered.at[pl.ds(part * PART, PART)]
-        return remote(ref, ref, fin_s.at[part], fin_r.at[part], sibling)
-
-    @pl.when(moves)
-    def _():
-        pl.semaphore_wait(barrier, PEERS - 1)
-        loss_copy.wait_recv()
-        loss_out[...] = loss_ret[...]
-        for part in range(PARTS):
-            rows = part_rows(part)
-            ret_copy(part).wait_recv()
-            grad_copy(part).wait_recv()
-            home = ret[rows, :].astype(jnp.float32)
-            seg_out[0, rows, :] = home
-            rs_send[rows, :] = (home + sib_grad[rows, :]).astype(RS_DTYPE)
-            for d in (4, 3, 5, 2, 6, 1, 7):
-                rs_copy(part, d).start()
-            rs_buf[part, peer] = rs_send[pl.ds(pl.multiple_of(part * PART + peer * PIECE, PIECE), PIECE), :]
-        for part in range(PARTS):
-            for d in range(1, PEERS):
-                rs_arrival(part, d).wait_recv()
-            reduced = rs_buf[part, 0].astype(jnp.float32)
-            for source in range(1, PEERS):
-                reduced += rs_buf[part, source].astype(jnp.float32)
-            gathered[pl.ds(pl.multiple_of(part * PART + peer * PIECE, PIECE), PIECE), :] = reduced.astype(jnp.bfloat16)
-            for d in (4, 3, 5, 2, 6, 1, 7):
-                ag_copy(part, d).start()
-        for part in range(PARTS):
-            for d in (1, 7, 2, 6, 3, 5, 4):
-                source = lax.rem(peer + PEERS - d, PEERS)
-                ag_arrival(part, source).wait_recv()
-            fin_copy(part).start()
-
-    @pl.when(stays)
-    def _():
-        for part in range(PARTS):
-            fin_copy(part).wait_recv()
 
     for way in range(2):
         for index in range(RING_COPIES):
@@ -403,11 +377,6 @@
     for dz, dc in others:
         total_copy(dz, dc).wait_send()
 
-    @pl.when(stays)
-    def _():
-        for part in range(PARTS):
-            grad_copy(part).wait_send()
-
     @pl.when(moves)
     def _():
         for which in range(CHUNKS):
@@ -416,13 +385,61 @@
         for copy in swap_raw():
             copy.wait_send()
         loss_copy.wait_send()
-        for part in range(PARTS):
-            ret_copy(part).wait_send()
-            for d in range(1, PEERS):
-                rs_copy(part, d).wait_send()
-            for d in range(1, PEERS):
+
+    def gathered_rows(part, owner):
+        return gathered.at[pl.ds(pl.multiple_of(part * PART + owner * PIECE, PIECE), PIECE)]
+
+    def ag_copy(part, d):
+        ref = gathered_rows(part, peer)
+        return remote(ref, ref, ag_s.at[part, d], ag_r.at[part, peer], at(z, x, lax.rem(peer + d, PEERS), core))
+
+    def ag_arrival(part, source):
+        ref = gathered_rows(part, source)
+        return remote(ref, ref, ag_s.at[part, 0], ag_r.at[part, source], sibling)
+
+    def fin_copy(part):
+        ref = gathered.at[pl.ds(part * PART, PART)]
+        return remote(ref, ref, fin_s.at[part], fin_r.at[part], sibling)
+
+    @pl.when(stays)
+    def _():
+        for part in range(PARTS):
+            for d in far_first[::-1]:
+                rs_arrival(part, lax.rem(peer + d, PEERS)).wait_recv()
+            for d in range(PEERS):
+                rs_arrival(part, PEERS + lax.rem(peer + d, PEERS)).wait_recv()
+            reduced = rs_buf[part, 0].astype(jnp.float32)
+            for source in range(1, 2 * PEERS):
+                reduced += rs_buf[part, source].astype(jnp.float32)
+            gathered[piece_rows(part, peer), :] = reduced.astype(jnp.bfloat16)
+            for d in far_first:
+                ag_copy(part, d).start()
+        for part in range(PARTS):
+            for d in far_first:
+                rs_copy(part, d, False).wait_send()
+        for part in range(PARTS):
+            for d in far_first[::-1]:
+                ag_arrival(part, lax.rem(peer + PEERS - d, PEERS)).wait_recv()
+            fin_copy(part).start()
+        for part in range(PARTS):
+            for d in far_first:
                 ag_copy(part, d).wait_send()
             fin_copy(part).wait_send()
+
+    @pl.when(moves)
+    def _():
+        loss_copy.wait_recv()
+        loss_out[...] = loss_ret[...]
+        for part in range(PARTS):
+            rows = part_rows(part)
+            ret_copy(part).wait_recv()
+            seg_out[0, rows, :] = ret[rows, :].astype(jnp.float32)
+        for part in range(PARTS):
+            ret_copy(part).wait_send()
+            for d in range(PEERS):
+                rs_copy(part, d, True).wait_send()
+        for part in range(PARTS):
+            fin_copy(part).wait_recv()
 
 
 def hand_over(loss_in, seg_in, sum_in, loss_out, seg_out, clip_out, wide, sems):
@@ -460,6 +477,7 @@
             pltpu.VMEM((ZS, E, PAIR), bf16),
             pltpu.VMEM((ZS, PAIR, ROWS), bf16),
             pltpu.VMEM((PAIR, 2 * ROWS), bf16),
+            pltpu.VMEM((E, PAIR), bf16),
             pltpu.VMEM((ZS, 2, 1, ROWS), f32),
             pltpu.VMEM((E, ROWS), bf16),
             pltpu.VMEM((ROWS, E), bf16),
@@ -475,22 +493,19 @@
             pltpu.VMEM((E, ROWS), f32),
             pltpu.VMEM((ROWS, E), bf16),
             pltpu.VMEM((ROWS, E), bf16),
-            pltpu.VMEM((ROWS, E), f32),
             pltpu.VMEM((1, ROWS), f32),
             pltpu.VMEM((1, ROWS), f32),
-            pltpu.VMEM((ROWS, E), RS_DTYPE),
-            pltpu.VMEM((PARTS, PEERS, PIECE, E), RS_DTYPE),
+            pltpu.VMEM((PARTS, 2 * PEERS, PIECE, E), bf16),
             dma((3,)),
             dma((CHUNKS + 3,)), dma((CHUNKS + 3,)),
             dma((2, RING_COPIES)), dma((2, RING_COPIES)),
             dma((ZS, CHUNKS)), dma((ZS, CHUNKS)),
             dma((ZS, 2)), dma((ZS, 2)),
             dma((PARTS + 1,)), dma((PARTS + 1,)),
-            dma((PARTS,)), dma((PARTS,)),
-            dma((PARTS, PEERS)), dma((PARTS, PEERS)),
+            dma((PARTS, PEERS)), dma((PARTS, 2 * PEERS)),
             dma((PARTS, PEERS)), dma((PARTS, PEERS)),
             dma((PARTS,)), dma((PARTS,)),
-            pltpu.SemaphoreType.REGULAR, pltpu.SemaphoreType.REGULAR,
+            pltpu.SemaphoreType.REGULAR, pltpu.SemaphoreType.REGULAR, pltpu.SemaphoreType.REGULAR,
         ],
         compiler_params=pltpu.CompilerParams(
             collective_id=0, has_side_effects=True, vmem_limit_bytes=56 * 2**20

time: 72.6 us -> 72 us (level)
  no operation moved by 1% of the time
where the time goes in v4:
time: 72 us; the launch traced here: 71.9 us
  Pallas kernels  71.3 us (99%)
    pallas_call x1, Pallas kernels, on_device(): pl.pallas_call(kernel, name='ntxent', out_shape=(pltpu.VMEM((1, ROWS), f3...  70.1 us

profile of v4, /device:TPU:1, one launch (start us, length us, event | category | flops | bytes accessed | tf_op | source)
XLA Modules:
  0.0 71.9 jit_solution(6021835388726352098)
XLA Ops:
  0.6 70.1 %ntxent.1 = (f32[1,384]{1,0:T(1,128)S(1)}, f32[1,384,512]{2,1,0:T(8,128)S(1)}, bf16[384,512]{1,0:T(8,128)(2,1)S(1)}) custom-call(bf16[384,512]{1,0:T(8,128)(2,1)} %clip_hbm.1, bf16[1,384,512]{2,1,0:T(8,128)(2,1)} %feat_hbm.1, s32[1,384]{1,0:T(1,128)} %pair_hbm.1), custom_call_target="tpu_custom_call" | custom-call | tf_op jit(solution)/shard_map/ntxent/pallas_call | solution.py:465
  70.8 1.2 %hand_over.1 = (f32[1,384]{1,0:T(1,128)}, f32[1,384,512]{2,1,0:T(8,128)}, f32[384,512]{1,0:T(8,128)}) custom-call(f32[1,384]{1,0:T(1,128)S(1)} %get-tuple-element.6.loss_in, f32[1,384,512]{2,1,0:T(8,128)S(1)} %get-tuple-element.7.seg_in, bf16[384,512]{1,0:T(8,128)(2,1)S(1)} %get-tuple-element.8.sum_in), custom_call_target="tpu_custom_call" | custom-call | tf_op jit(solution)/shard_map/hand_over/pallas_call | solution.py:514

commit v5 on v4

--- a/solution.py
+++ b/solution.py
@@ -43,7 +43,7 @@
     pull_one, pull_pos, acc, summed_t, ret_stage, ret, loss_stage, loss_ret,
     rs_buf,
     load_s, swap_s, swap_r, ring_s, ring_r, sib_s, sib_r, tot_s, tot_r, ret_s, ret_r,
-    rs_s, rs_r, ag_s, ag_r, fin_s, fin_r, near, go, peers_in,
+    rs_s, rs_r, ag_s, ag_r, last_s, last_r, fin_s, fin_r, near, go, peers_in,
 ):
     clip = lax.axis_index("clip")
     tm = lax.axis_index("tm")
@@ -79,19 +79,27 @@
     def _():
         greet(sibling, barrier)
 
-    loads = [
-        pltpu.make_async_copy(clip_hbm, home_clip, load_s.at[0]),
-        pltpu.make_async_copy(feat_hbm.at[0], home_feat, load_s.at[1]),
-    ]
-    pair_load = pltpu.make_async_copy(pair_hbm, partner, load_s.at[2])
-    for load in loads:
-        load.start()
-    for load in loads:
-        load.wait()
-
-    summed = home_clip[...].astype(jnp.float32) + home_feat[...].astype(jnp.float32)
-    factor = lax.rsqrt(jnp.sum(summed * summed, 1, keepdims=True) + E * norm_eps)
-    unit = (summed * factor).astype(jnp.bfloat16)
+    chunk_order = [c for o in range(CHUNKS // 2) for c in (o, CHUNKS - 1 - o)]
+    pair_load = pltpu.make_async_copy(pair_hbm, partner, load_s.at[2, 0])
+
+    def chunk_loads(which):
+        rows = pl.ds(which * CHUNK, CHUNK)
+        return [
+            pltpu.make_async_copy(clip_hbm.at[rows], home_clip.at[rows], load_s.at[0, which]),
+            pltpu.make_async_copy(feat_hbm.at[0, rows], home_feat.at[rows], load_s.at[1, which]),
+        ]
+
+    for which in chunk_order:
+        for load in chunk_loads(which):
+            load.start()
+
+    def unit_chunk(which):
+        rows = slice(which * CHUNK, (which + 1) * CHUNK)
+        for load in chunk_loads(which):
+            load.wait()
+        summed = home_clip[rows, :].astype(jnp.float32) + home_feat[rows, :].astype(jnp.float32)
+        factor = lax.rsqrt(jnp.sum(summed * summed, 1, keepdims=True) + E * norm_eps)
+        return (summed * factor).astype(jnp.bfloat16)
 
     def chunk_of(zz, block, which):
         return u_all.at[zz, pl.ds(pl.multiple_of(block * ROWS + which * CHUNK, CHUNK), CHUNK)]
@@ -125,31 +133,37 @@
         ref = chunk_of(source, 1 - core, which)
         return remote(ref, ref, sib_s.at[source, which], sib_r.at[source, which], sibling)
 
-    swap_order = [c for o in range(CHUNKS // 2) for c in (o, CHUNKS - 1 - o)]
 
     @pl.when(stays)
     def _():
         pair_load.start()
-        u_all[z, pl.ds(pl.multiple_of(core * ROWS, ROWS), ROWS), :] = unit
         pl.semaphore_wait(barrier, 4)
         for device in neighbours:
             greet(device, near)
-        for order in range(CHUNKS):
+        for order in range(CHUNKS // 2):
+            for way in range(2):
+                which = order_chunk(way, order)
+                rows = pl.ds(pl.multiple_of(core * ROWS + which * CHUNK, CHUNK), CHUNK)
+                u_all[z, rows, :] = unit_chunk(which)
+                ring_copy(way, 0, order).start()
+            if order == 0:
+                pl.semaphore_wait(near, 3)
+                greet(sibling, go)
+        for order in range(CHUNKS // 2, CHUNKS):
             for way in range(2):
                 ring_copy(way, 0, order).start()
-        for which in swap_order:
+        for which in chunk_order:
             sib_copy(z, which).start()
-        pl.semaphore_wait(near, 3)
-        greet(sibling, go)
         raw_clip[...] = home_clip[...]
         raw_feat[...] = home_feat[...]
         pair_load.wait()
 
     @pl.when(moves)
     def _():
-        stage[...] = unit
+        for which in chunk_order:
+            stage[which * CHUNK:(which + 1) * CHUNK, :] = unit_chunk(which)
         pl.semaphore_wait(go, 1)
-        for which in swap_order:
+        for which in chunk_order:
             swap_unit(which, x).start()
         swap_pair.start()
         for order in range(CHUNKS // 2):
@@ -176,12 +190,14 @@
         hop = (step + 1) // 2
         return ring(jnp.where(lax.rem(step, 2) == 1, -hop, hop))
 
-    def score_part(zz):
-        score = dot(u_all[zz], unit_t[...])
+    def score_part(zz, block):
+        rows = pl.ds(pl.multiple_of(block * ROWS, ROWS), ROWS)
+        score = dot(u_all[zz, rows, :], unit_t[...])
+        ids = lax.broadcasted_iota(jnp.int32, (ROWS, ROWS), 0) + (zz * PAIR + block * ROWS)
         own = lax.broadcasted_iota(jnp.int32, (1, ROWS), 1) + (z * PAIR + core * ROWS)
-        expo = jnp.where(column_ids(zz) != own, jnp.exp2(score * exp2_scale - exp2_scale), 0.0)
+        expo = jnp.where(ids != own, jnp.exp2(score * exp2_scale - exp2_scale), 0.0)
         totals[...] += jnp.sum(expo, 0, keepdims=True)
-        expo_all[zz] = expo.astype(jnp.bfloat16)
+        expo_all[zz, rows, :] = expo.astype(jnp.bfloat16)
 
     def pull_part(zz):
         ut_all[zz] = u_all[zz].T
@@ -248,9 +264,10 @@
             summed_t[...] = (raw_clip[...].astype(jnp.float32) + raw_feat[...].astype(jnp.float32)).T
 
         zz = block_of(step)
+        score_part(zz, core)
         for which in range(CHUNKS):
             sib_arrival(zz, which).wait_recv()
-        score_part(zz)
+        score_part(zz, 1 - core)
         return carry
 
     lax.fori_loop(0, ZS, gather_step, 0)
@@ -306,12 +323,14 @@
         return carry
 
     acc[...] += second(z, True)
-    lax.fori_loop(1, 4, second_hop, 0)
+    for hop in range(1, 4):
+        second_hop(hop, 0)
     last = ring(4)
     total_arrival(last, core).wait_recv()
     total_arrival(last, 1 - core).wait_recv()
     scale = 1.0 / jnp.concatenate([tot_all[last, 0], tot_all[last, 1]], 1)
-    scaled_last[...] = (ut_all[last].astype(jnp.float32) * scale).astype(jnp.bfloat16)
+    scaled = (ut_all[last].astype(jnp.float32) * scale).astype(jnp.bfloat16)
+    scaled_last[...] = scaled
 
     def part_rows(part):
         return slice(part * PART, (part + 1) * PART)
@@ -396,6 +415,14 @@
     def ag_arrival(part, source):
         ref = gathered_rows(part, source)
         return remote(ref, ref, ag_s.at[part, 0], ag_r.at[part, source], sibling)
+
+    def last_copy(d):
+        ref = gathered_rows(PARTS - 1, peer)
+        return remote(ref, ref, last_s.at[d], last_r.at[peer], at(z, x, lax.rem(peer + d, PEERS), 1 - core))
+
+    def last_arrival(source):
+        ref = gathered_rows(PARTS - 1, source)
+        return remote(ref, ref, last_s.at[0], last_r.at[source], sibling)
 
     def fin_copy(part):
         ref = gathered.at[pl.ds(part * PART, PART)]
@@ -414,17 +441,25 @@
             gathered[piece_rows(part, peer), :] = reduced.astype(jnp.bfloat16)
             for d in far_first:
                 ag_copy(part, d).start()
+                if part == PARTS - 1:
+                    last_copy(d).start()
+            if part == PARTS - 1:
+                last_copy(0).start()
         for part in range(PARTS):
             for d in far_first:
                 rs_copy(part, d, False).wait_send()
         for part in range(PARTS):
             for d in far_first[::-1]:
                 ag_arrival(part, lax.rem(peer + PEERS - d, PEERS)).wait_recv()
-            fin_copy(part).start()
+            if part < PARTS - 1:
+                fin_copy(part).start()
         for part in range(PARTS):
             for d in far_first:
                 ag_copy(part, d).wait_send()
-            fin_copy(part).wait_send()
+            if part < PARTS - 1:
+                fin_copy(part).wait_send()
+        for d in range(PEERS):
+            last_copy(d).wait_send()
 
     @pl.when(moves)
     def _():
@@ -439,7 +474,10 @@
             for d in range(PEERS):
                 rs_copy(part, d, True).wait_send()
         for part in range(PARTS):
-            fin_copy(part).wait_recv()
+            if part < PARTS - 1:
+                fin_copy(part).wait_recv()
+        for d in (0,) + far_first[::-1]:
+            last_arrival(lax.rem(peer + PEERS - d, PEERS)).wait_recv()
 
 
 def hand_over(loss_in, seg_in, sum_in, loss_out, seg_out, clip_out, wide, sems):
@@ -496,7 +534,7 @@
             pltpu.VMEM((1, ROWS), f32),
             pltpu.VMEM((1, ROWS), f32),
             pltpu.VMEM((PARTS, 2 * PEERS, PIECE, E), bf16),
-            dma((3,)),
+            dma((3, CHUNKS)),
             dma((CHUNKS + 3,)), dma((CHUNKS + 3,)),
             dma((2, RING_COPIES)), dma((2, RING_COPIES)),
             dma((ZS, CHUNKS)), dma((ZS, CHUNKS)),
@@ -504,6 +542,7 @@
             dma((PARTS + 1,)), dma((PARTS + 1,)),
             dma((PARTS, PEERS)), dma((PARTS, 2 * PEERS)),
             dma((PARTS, PEERS)), dma((PARTS, PEERS)),
+            dma((PEERS,)), dma((PEERS,)),
             dma((PARTS,)), dma((PARTS,)),
             pltpu.SemaphoreType.REGULAR, pltpu.SemaphoreType.REGULAR, pltpu.SemaphoreType.REGULAR,
         ],

time: 72 us -> 71.6 us (level)
  no operation moved by 1% of the time
where the time goes in v5:
time: 71.6 us; the launch traced here: 71.5 us
  Pallas kernels  70.9 us (99%)
    pallas_call x1, Pallas kernels, on_device(): pl.pallas_call(kernel, name='ntxent', out_shape=(pltpu.VMEM((1, ROWS), f3...  69.7 us

profile of v5, /device:TPU:1, one launch (start us, length us, event | category | flops | bytes accessed | tf_op | source)
XLA Modules:
  0.0 71.5 jit_solution(8438364555267246572)
XLA Ops:
  0.6 69.7 %ntxent.1 = (f32[1,384]{1,0:T(1,128)S(1)}, f32[1,384,512]{2,1,0:T(8,128)S(1)}, bf16[384,512]{1,0:T(8,128)(2,1)S(1)}) custom-call(bf16[384,512]{1,0:T(8,128)(2,1)} %clip_hbm.1, bf16[1,384,512]{2,1,0:T(8,128)(2,1)} %feat_hbm.1, s32[1,384]{1,0:T(1,128)} %pair_hbm.1), custom_call_target="tpu_custom_call" | custom-call | tf_op jit(solution)/shard_map/ntxent/pallas_call | solution.py:503
  70.4 1.2 %hand_over.1 = (f32[1,384]{1,0:T(1,128)}, f32[1,384,512]{2,1,0:T(8,128)}, f32[384,512]{1,0:T(8,128)}) custom-call(f32[1,384]{1,0:T(1,128)S(1)} %get-tuple-element.6.loss_in, f32[1,384,512]{2,1,0:T(8,128)S(1)} %get-tuple-element.7.seg_in, bf16[384,512]{1,0:T(8,128)(2,1)S(1)} %get-tuple-element.8.sum_in), custom_call_target="tpu_custom_call" | custom-call | tf_op jit(solution)/shard_map/hand_over/pallas_call | solution.py:553

commit v6 on v5

--- a/solution.py
+++ b/solution.py
@@ -484,12 +484,14 @@
     copies = [
         pltpu.make_async_copy(seg_in, seg_out, sems.at[0]),
         pltpu.make_async_copy(loss_in, loss_out, sems.at[1]),
-        pltpu.make_async_copy(wide, clip_out, sems.at[2]),
     ]
-    for copy in copies[:2]:
+    for copy in copies:
         copy.start()
-    wide[...] = sum_in[...].astype(jnp.float32)
-    copies[2].start()
+    for part in range(PARTS):
+        rows = pl.ds(part * PART, PART)
+        wide[rows, :] = sum_in[rows, :].astype(jnp.float32)
+        copies.append(pltpu.make_async_copy(wide.at[rows], clip_out.at[rows], sems.at[2 + part]))
+        copies[-1].start()
     for copy in copies:
         copy.wait()
 
@@ -560,7 +562,7 @@
         ),
         in_specs=[vmem] * 3,
         out_specs=(anywhere,) * 3,
-        scratch_shapes=[pltpu.VMEM((ROWS, E), f32), dma((3,))],
+        scratch_shapes=[pltpu.VMEM((ROWS, E), f32), dma((2 + PARTS,))],
         compiler_params=pltpu.CompilerParams(vmem_limit_bytes=4 * 2**20),
     )(loss, seg, total)
 

time: 71.6 us -> 71.6 us (level)
  no operation moved by 1% of the time
where the time goes in v6:
time: 71.6 us; the launch traced here: 71.5 us
  Pallas kernels  70.9 us (99%)
    pallas_call x1, Pallas kernels, on_device(): pl.pallas_call(kernel, name='ntxent', out_shape=(pltpu.VMEM((1, ROWS), f3...  69.7 us

profile of v6, /device:TPU:1, one launch (start us, length us, event | category | flops | bytes accessed | tf_op | source)
XLA Modules:
  0.0 71.5 jit_solution(1300058827764850774)
XLA Ops:
  0.6 69.7 %ntxent.1 = (f32[1,384]{1,0:T(1,128)S(1)}, f32[1,384,512]{2,1,0:T(8,128)S(1)}, bf16[384,512]{1,0:T(8,128)(2,1)S(1)}) custom-call(bf16[384,512]{1,0:T(8,128)(2,1)} %clip_hbm.1, bf16[1,384,512]{2,1,0:T(8,128)(2,1)} %feat_hbm.1, s32[1,384]{1,0:T(1,128)} %pair_hbm.1), custom_call_target="tpu_custom_call" | custom-call | tf_op jit(solution)/shard_map/ntxent/pallas_call | solution.py:505
  70.4 1.2 %hand_over.1 = (f32[1,384]{1,0:T(1,128)}, f32[1,384,512]{2,1,0:T(8,128)}, f32[384,512]{1,0:T(8,128)}) custom-call(f32[1,384]{1,0:T(1,128)S(1)} %get-tuple-element.6.loss_in, f32[1,384,512]{2,1,0:T(8,128)S(1)} %get-tuple-element.7.seg_in, bf16[384,512]{1,0:T(8,128)(2,1)S(1)} %get-tuple-element.8.sum_in), custom_call_target="tpu_custom_call" | custom-call | tf_op jit(solution)/shard_map/hand_over/pallas_call | solution.py:555
